TPU v7x, 256 devices: a whole 4x4x8 slice. The times are simulated.
256 devices in a mesh: forest: 8 (over x, core), tile: 32 (over z, y).
Axes of the slice: x: 4, y: 4, z: 8, core: 2. Of those that a mesh axis runs over, the one named last changes fastest.
Arguments:
- left_panels: bfloat16 [8, 256, 2, 256, 256], P('forest', 'tile'), may hold values from -4 to 4
- right_panels: bfloat16 [8, 256, 1, 256, 256], P('forest', 'tile'), may hold values from -0.375 to 0.375
- dest_owner: int32 [8, 256, 1], P('forest', 'tile'), may hold values from 0 to 31; in each aligned block of 8 rows (0 to 7, 8 to 15, ..., all dimensions but the last counted through in order) at most 2 rows name the same one
- tile_slot: int32 [8, 256], P('forest', 'tile'), may hold values from 0 to 1
- frontal_tiles: float32 [64, 2, 256, 256], P('tile', None, 'forest'), may hold values from -6 to 6
- diag_inverse: float32 [256, 256], replicated, as said below
- reader_tile: int32 [128], replicated, may hold values from 0 to 63
Outputs:
- ancestor: float32 [64, 2, 256, 256], P('tile', None, 'forest')
- panel_read: float32 [128, 2, 256, 256], P('tile', None, 'forest')
Inputs may be any that keep to these rules, and one draw needn't show every extreme that they name: `dest_owner`: among the pairs of one device at most 2 name the same owner, and some device has exactly 2 for one owner. `diag_inverse`: an upper triangular matrix with a positive diagonal.
All inputs are finite; a program needn't handle non-finite values.
Results may differ from a plain program's by a relative error of at most 0.0003.
Values may be sent and summed in bfloat16 or wider, within the bound.
A program may use at most 192 MiB of HBM per device.

v0:
```python
import jax
import jax.numpy as jnp
from jax import lax
from jax.sharding import PartitionSpec as P

READS = 4


def per_device(
    left_panels, right_panels, dest_owner, tile_slot, frontal_tiles, diag_inverse, reader_tile
):
    left_block = left_panels[0]
    right_block = right_panels[0]
    owners = dest_owner[0, :, 0]
    slot_index = tile_slot[0]
    tile_count = lax.axis_size("tile")
    pair_count = left_block.shape[0]
    left_depth = left_block.shape[1]
    right_depth = right_block.shape[1]
    tile_depth = left_depth * right_depth
    block_width = left_block.shape[2]
    per_dev = frontal_tiles.shape[0]
    capacity = max(2, 2 * pair_count // tile_count)
    owner_hot = (owners[:, None] == jnp.arange(tile_count, dtype=jnp.int32)[None, :]).astype(
        jnp.int32
    )
    arrival = jnp.sum(jnp.cumsum(owner_hot, axis=0) * owner_hot, axis=1) - 1
    placed_at = owners * capacity + arrival
    slot_count = tile_count * capacity
    send_left = (
        jnp.zeros((slot_count, left_depth, block_width, block_width), jnp.bfloat16)
        .at[placed_at]
        .set(left_block)
    )
    send_right = (
        jnp.zeros((slot_count, right_depth, block_width, block_width), jnp.bfloat16)
        .at[placed_at]
        .set(right_block)
    )
    codes_sent = (
        jnp.full((slot_count,), -1.0, jnp.float32).at[placed_at].set(slot_index.astype(jnp.float32))
    )
    send_left = send_left.reshape(tile_count, capacity, left_depth, block_width, block_width)
    send_right = send_right.reshape(tile_count, capacity, right_depth, block_width, block_width)
    codes_sent = codes_sent.astype(jnp.bfloat16).reshape(tile_count, capacity)
    left_piece = lax.all_to_all(send_left, "tile", split_axis=0, concat_axis=0, tiled=True)
    right_piece = lax.all_to_all(send_right, "tile", split_axis=0, concat_axis=0, tiled=True)
    code_piece = lax.all_to_all(codes_sent, "tile", split_axis=0, concat_axis=0, tiled=True)
    product = jnp.einsum(
        "smaij,smcjk->smacik", left_piece, right_piece, preferred_element_type=jnp.float32
    )
    products = product
    products = products.reshape(-1, tile_depth, block_width, block_width) / left_depth
    code_index = code_piece.astype(jnp.float32).reshape(-1).astype(jnp.int32)
    code_index = jnp.where(code_index < 0, per_dev, code_index)
    updates = (
        jnp.zeros((per_dev, tile_depth, block_width, block_width), jnp.float32)
        .at[code_index]
        .add(products, mode="drop")
    )
    reduced = lax.psum_scatter(updates, "forest", scatter_dimension=2, tiled=True)
    schur_tile = frontal_tiles - reduced
    panel_tile = jnp.einsum(
        "qtrj,jk->qtrk", schur_tile, diag_inverse, precision=lax.Precision.HIGHEST
    )
    gathered = lax.all_gather(panel_tile, "tile", axis=0, tiled=True)
    my_reads = lax.dynamic_slice_in_dim(reader_tile, lax.axis_index("tile") * READS, READS, 0)
    picked = jnp.take(gathered, my_reads, axis=0)
    return (schur_tile, picked)


def solution(mesh):
    placed = (
        P("forest", "tile", None, None, None),
        P("forest", "tile", None, None, None),
        P("forest", "tile", None),
        P("forest", "tile"),
        P("tile", None, "forest", None),
        P(),
        P(),
    )
    return jax.shard_map(
        per_device,
        mesh=mesh,
        in_specs=placed,
        out_specs=(P("tile", None, "forest", None), P("tile", None, "forest", None)),
        check_vma=False,
    )
```

profile of v0, /device:TPU:1, one launch (start us, length us, event | category | flops | bytes accessed | tf_op | source)
XLA Modules:
  0.0 870.2 jit_solution(13052918613229153396)
XLA Ops:
  7.2 0.0 copy-start
  7.2 0.8 fusion.3
  8.0 0.8 select_reduce_fusion
  8.8 0.7 fusion.4
  9.5 0.7 convert_bitcast_fusion
  10.1 0.6 scatter_custom_fusion
  10.7 0.7 all_to_all.16
  11.5 12.0 %all-to-all-start = ((bf16[32,1,2]{2,1,0:T(2,128)(2,1)}), bf16[32,1,2]{2,1,0:T(2,128)(2,1)S(1)}, u32[]{:S(2)}, u32[]{:S(2)}) async-start(bf16[32,1,2]{2,1,0:T(2,128)(2,1)} %all_to_all.16), calls=%async_computation | async-start | bytes 32768 | tf_op jit(solution)/shard_map/all_to_all | solution.py:48
  23.5 4.2 broadcast.103
  27.8 3.3 scatter_fusion
  31.0 11.9 %copy.16 = bf16[32,2,1,256,256]{3,4,1,2,0:T(8,128)(2,1)} copy(bf16[32,2,1,256,256]{4,3,1,0,2:T(8,128)(2,1)} %bitcast.37) | data formatting | bytes 16777216 | tf_op jit(solution)/shard_map/reshape | solution.py:44
  42.9 0.0 copy-start.2
  42.9 0.0 all-to-all-done
  42.9 9.5 %all-to-all-start.1 = ((bf16[32,2,1,256,256]{3,4,1,2,0:T(8,128)(2,1)}), bf16[32,2,1,256,256]{3,4,1,2,0:T(8,128)(2,1)}, u32[]{:S(2)}, u32[]{:S(2)}) async-start(bf16[32,2,1,256,256]{3,4,1,2,0:T(8,128)(2,1)} %copy.16), calls=%async_computation.1 | async-start | bytes 16777216 | tf_op jit(solution)/shard_map/all_to_all | solution.py:47
  52.4 5.9 broadcast_in_dim.37
  58.3 0.0 copy-done.2
  58.3 5.0 scatter_fusion.1
  63.4 180.3 %all-to-all-done.1 = bf16[32,2,1,256,256]{3,4,1,2,0:T(8,128)(2,1)} async-done(((bf16[32,2,1,256,256]{3,4,1,2,0:T(8,128)(2,1)}), bf16[32,2,1,256,256]{3,4,1,2,0:T(8,128)(2,1)}, u32[]{:S(2)}, u32[]{:S(2)}) %all-to-all-start.1) | async-done | bytes 8388640 | tf_op jit(solution)/shard_map/all_to_all | solution.py:47
  243.7 6.3 all-to-all-start.2
  249.9 0.0 reduce-scatter.2.cloned.1.call-start
  250.0 0.1 convert_reduce_fusion
  250.1 0.1 convert_element_type.43
  250.2 386.7 %all-to-all-done.2 = bf16[32,2,2,256,256]{4,3,2,1,0:T(8,128)(2,1)} async-done(((bf16[32,2,2,256,256]{4,3,2,1,0:T(8,128)(2,1)}), bf16[32,2,2,256,256]{4,3,2,1,0:T(8,128)(2,1)}, u32[]{:S(2)}, u32[]{:S(2)}) %all-to-all-start.2) | async-done | bytes 16777248 | tf_op jit(solution)/shard_map/all_to_all | solution.py:46
  636.9 19.7 %broadcast_multiply_fusion = f32[32,2,256,2,256]{4,2,3,1,0:T(8,128)} fusion(bf16[32,2,2,256,256]{4,3,2,1,0:T(8,128)(2,1)} %all-to-all-done.2, bf16[32,2,1,256,256]{3,4,1,2,0:T(8,128)(2,1)} %all-to-all-done.1), kind=kOutput, calls=%fused_computation.5 | convolution fusion | flops 4303355904 | bytes 58720256 | tf_op jit(solution)/shard_map/smaij,smcjk->smacik/dot_general | solution.py:49
  656.6 33.4 %copy.17 = f32[64,2,256,256]{3,2,1,0:T(8,128)} copy(f32[64,2,256,256]{2,3,1,0:T(8,128)} %bitcast.35) | data formatting | bytes 67108864 | tf_op jit(solution)/shard_map/div | solution.py:53
  690.0 0.1 broadcast_in_dim.33
  690.1 0.0 copy-start.4
  690.1 0.0 copy-start.5
  690.1 40.7 %scatter_fusion.2 = f32[2,2,256,256]{3,2,1,0:T(8,128)S(1)} fusion(f32[2,2,256,256]{3,2,1,0:T(8,128)S(1)} %broadcast_in_dim.33, s32[64]{0:T(128)S(1)} %fusion.5, f32[64,2,256,256]{3,2,1,0:T(8,128)} %copy.17), kind=kCustom, calls=%fused_computation.4 | custom fusion | flops 8388608 | bytes 100663552 | tf_op jit(solution)/shard_map/scatter-add | solution.py:59
  730.8 0.0 copy-start.1
  730.8 1.0 copy-done.1
  731.8 0.0 reduce-scatter.2.cloned.1.call-update
  731.8 0.0 all-gather.2.cloned.1.call-start
  731.9 44.3 %reduce-scatter.2.cloned.1.call-done = f32[2,2,32,256]{3,2,1,0:T(8,128)} async-done(((f32[2,2,256,256]{3,2,1,0:T(8,128)}), f32[2,2,32,256]{3,2,1,0:T(8,128)}) %reduce-scatter.2.cloned.1.call-update) | async-done | bytes 131088 | tf_op jit(solution)/shard_map/reduce_scatter | solution.py:61
  776.2 0.0 copy-done.4
  776.2 0.9 sub.10
  777.1 0.0 copy-done
  777.1 0.0 copy-start.3
  777.1 0.9 fusion.1
  778.1 0.0 all-gather.2.cloned.1.call-update
  778.1 0.0 copy-done.5
  778.1 0.1 compare_and_fusion
  778.2 81.6 %all-gather.2.cloned.1.call-done = f32[64,2,32,256]{3,2,1,0:T(8,128)} async-done(((f32[2,2,32,256]{3,2,1,0:T(8,128)}), f32[64,2,32,256]{3,2,1,0:T(8,128)}) %all-gather.2.cloned.1.call-update) | async-done | bytes 4194320 | tf_op jit(solution)/shard_map/all_gather | solution.py:66
  859.8 2.7 gather_fusion
  862.6 0.8 broadcast_select_fusion
  863.4 0.0 copy-done.3
  (4 shorter events, 0.0 us)
Async XLA Ops:
  7.2 770.0 %copy-start = (f32[256,256]{1,0:T(8,128)S(1)}, f32[256,256]{1,0:T(8,128)}, u32[]{:S(2)}) copy-start(f32[256,256]{1,0:T(8,128)} %param.12) | copy-start | bytes 786436
  11.5 31.5 %all-to-all-start = ((bf16[32,1,2]{2,1,0:T(2,128)(2,1)}), bf16[32,1,2]{2,1,0:T(2,128)(2,1)S(1)}, u32[]{:S(2)}, u32[]{:S(2)}) async-start(bf16[32,1,2]{2,1,0:T(2,128)(2,1)} %all_to_all.16), calls=%async_computation | async-start | bytes 32768 | tf_op jit(solution)/shard_map/all_to_all | solution.py:48
  42.9 15.4 %copy-start.2 = (bf16[1,8,2,256,256]{4,3,2,1,0:T(8,128)(2,1)S(1)}, bf16[1,8,2,256,256]{4,3,2,1,0:T(8,128)(2,1)}, u32[]{:S(2)}) copy-start(bf16[1,8,2,256,256]{4,3,2,1,0:T(8,128)(2,1)} %param.7) | copy-start | bytes 6291460
  42.9 200.7 %all-to-all-start.1 = ((bf16[32,2,1,256,256]{3,4,1,2,0:T(8,128)(2,1)}), bf16[32,2,1,256,256]{3,4,1,2,0:T(8,128)(2,1)}, u32[]{:S(2)}, u32[]{:S(2)}) async-start(bf16[32,2,1,256,256]{3,4,1,2,0:T(8,128)(2,1)} %copy.16), calls=%async_computation.1 | async-start | bytes 16777216 | tf_op jit(solution)/shard_map/all_to_all | solution.py:47
  243.7 393.3 %all-to-all-start.2 = ((bf16[32,2,2,256,256]{4,3,2,1,0:T(8,128)(2,1)}), bf16[32,2,2,256,256]{4,3,2,1,0:T(8,128)(2,1)}, u32[]{:S(2)}, u32[]{:S(2)}) async-start(bf16[32,2,2,256,256]{4,3,2,1,0:T(8,128)(2,1)} %bitcast.36), calls=%async_computation.2 | async-start | bytes 33554432 | tf_op jit(solution)/shard_map/all_to_all | solution.py:46
  249.9 526.2 %reduce-scatter.2.cloned.1.call-start = ((), (), s32[]{:S(2)}) async-start(), calls=%async_computation.4 | async-start | bytes 1179648 | tf_op jit(solution)/shard_map/reduce_scatter | solution.py:61
  690.1 86.1 %copy-start.4 = (f32[2,2,32,256]{3,2,1,0:T(8,128)S(1)}, f32[2,2,32,256]{3,2,1,0:T(8,128)}, u32[]{:S(2)}) copy-start(f32[2,2,32,256]{3,2,1,0:T(8,128)} %param.11) | copy-start | bytes 393220
  690.1 88.0 %copy-start.5 = (s32[128]{0:T(128)S(1)}, s32[128]{0:T(128)}, u32[]{:S(2)}) copy-start(s32[128]{0:T(128)} %param.13) | copy-start | bytes 1540
  730.8 1.0 copy-start.1
  731.8 128.0 %all-gather.2.cloned.1.call-start = ((), (), s32[]{:S(2)}) async-start(), calls=%async_computation.5 | async-start | bytes 4325376 | tf_op jit(solution)/shard_map/all_gather | solution.py:66
  777.1 86.3 %copy-start.3 = (f32[2,2,32,256]{3,2,1,0:T(8,128)}, f32[2,2,32,256]{3,2,1,0:T(8,128)S(1)}, u32[]{:S(2)}) copy-start(f32[2,2,32,256]{3,2,1,0:T(8,128)S(1)} %sub.10) | copy-start | bytes 393220
Sparse Core Ops, SparseCore 0:
  731.9 44.2 reduce-scatter.1
  779.3 80.4 all-gather.1
where the time goes:
time: 874 us; the launch traced here: 870 us
  waiting for transfers between devices  693 us (79%)
  local copies, waits for them, and re-layouts  69.1 us (8%)
  other arithmetic  45.5 us (5%)
  starting transfers between devices  27.9 us (3%)
  matrix products  20.6 us (2%)
  between operations  14.2 us (2%)
    all_to_all x1, waiting for transfers between devices, per_device(): lax.all_to_all(send_left, 'tile', split_axis=0, concat_axis=0, tiled=True)  387 us
    all_to_all x1, waiting for transfers between devices, per_device(): lax.all_to_all(send_right, 'tile', split_axis=0, concat_axis=0, tiled=True)  180 us
    all_gather x1, waiting for transfers between devices, per_device(): gathered = lax.all_gather(panel_tile, 'tile', axis=0, tiled=True)  81.6 us
    reduce_scatter x1, waiting for transfers between devices, per_device(): lax.psum_scatter(updates, 'forest', scatter_dimension=2, tiled=True)  44.3 us
    scatter-add x1, other arithmetic, per_device(): updates = jnp.zeros((per_dev, tile_depth, block_width, block_width), jnp....  40.7 us
    div x1, local copies, waits for them, and re-layouts, per_device(): products.reshape(-1, tile_depth, block_width, block_width) / left_depth  33.4 us
    dot_general x1, matrix products, per_device(): jnp.einsum('smaij,smcjk->smacik', left_piece, right_piece, preferred_elem...  19.7 us
  transfers between devices with their start and end apart: 5, of which 4 were waited for; matrix products, arithmetic and copies ran while one was open for 4% of the time, Pallas kernels for 0%

commit v1 on v0

v1 whole, which is shorter than its diff:
```python
import jax
import jax.numpy as jnp
from jax import lax
from jax.sharding import PartitionSpec as P


def per_device(
    left_panels, right_panels, dest_owner, tile_slot, frontal_tiles, diag_inverse, reader_tile
):
    forest_count = lax.axis_size("forest")
    tile_count = lax.axis_size("tile")
    per_dev = frontal_tiles.shape[0]
    group_count = tile_count * per_dev
    left_block = left_panels[0]
    right_block = right_panels[0, :, 0]
    pairs, depth, width = left_block.shape[:3]
    rows = width // forest_count
    group = dest_owner[0, :, 0] * per_dev + tile_slot[0]

    with jax.named_scope("products"):
        products = jnp.einsum(
            "kaij,kjl->kail", left_block, right_block, preferred_element_type=jnp.float32
        )
        products = products.reshape(pairs, depth, forest_count, rows, width)
        products = products.transpose(2, 0, 1, 3, 4)
    with jax.named_scope("to_row_owners"):
        groups = lax.all_gather(group, "forest", axis=0, tiled=True)
        pieces = lax.all_to_all(products, "forest", split_axis=0, concat_axis=0, tiled=True)
    with jax.named_scope("sum_by_group"):
        pieces = pieces.reshape(forest_count * pairs, depth * rows * width)
        hot = jnp.where(
            groups[None, :] == jnp.arange(group_count, dtype=jnp.int32)[:, None], 1.0 / depth, 0.0
        ).astype(jnp.float32)
        updates = jnp.dot(hot, pieces, precision=lax.Precision.HIGHEST)
        updates = updates.reshape(group_count, depth, rows, width)
        reduced = lax.psum_scatter(updates, "tile", scatter_dimension=0, tiled=True)
    with jax.named_scope("solve"):
        ancestor = frontal_tiles - reduced
        panel = jnp.einsum(
            "qtrj,jk->qtrk", ancestor, diag_inverse, precision=lax.Precision.HIGHEST
        )
    with jax.named_scope("reads"):
        gathered = lax.all_gather(panel, "tile", axis=0, tiled=True)
        reads = reader_tile.shape[0] // tile_count
        first = lax.axis_index("tile") * reads
        picked = []
        for i in range(reads):
            at = lax.dynamic_index_in_dim(reader_tile, first + i, 0, keepdims=False)
            picked.append(lax.dynamic_slice_in_dim(gathered, at, 1, 0))
        picked = jnp.concatenate(picked, axis=0)
    return ancestor, picked


def solution(mesh):
    placed = (
        P("forest", "tile", None, None, None),
        P("forest", "tile", None, None, None),
        P("forest", "tile", None),
        P("forest", "tile"),
        P("tile", None, "forest", None),
        P(),
        P(),
    )
    return jax.shard_map(
        per_device,
        mesh=mesh,
        in_specs=placed,
        out_specs=(P("tile", None, "forest", None), P("tile", None, "forest", None)),
        check_vma=False,
    )
```

time: 874 us -> 404 us (0.46)
  waiting for transfers between devices: 693 us -> 293 us
  local copies, waits for them, and re-layouts: 69.1 us -> 18.9 us
  blocking collectives: 0 us -> 49.2 us
  other arithmetic: 45.5 us -> 1.75 us
  starting transfers between devices: 27.9 us -> 7.85 us
  matrix products: 20.6 us -> 8.83 us
    all_to_all x3 -> x1, waiting for transfers between devices: 567 us -> 0.01 us  [per_device(): lax.all_to_all(products, 'forest', split_axis=0, concat_axis=0, tiled=True)]
    reduce_scatter x1, waiting for transfers between devices: 44.3 us -> 217 us  [per_device(): reduced = lax.psum_scatter(updates, 'tile', scatter_dimension=0, tiled=True)]
    unnamed x0 -> x1, blocking collectives: none -> 49.2 us
    scatter-add x1 -> x0, other arithmetic: 40.7 us -> none  [per_device(): updates = jnp.zeros((per_dev, tile_depth, block_width, block_width), jnp....]
    div x1 -> x0, local copies, waits for them, and re-layouts: 33.4 us -> none  [per_device(): products.reshape(-1, tile_depth, block_width, block_width) / left_depth]
    all_to_all x3 -> x1, starting transfers between devices: 27.8 us -> 7.8 us  [per_device(): lax.all_to_all(products, 'forest', split_axis=0, concat_axis=0, tiled=True)]
    dot_general x2 -> x3, matrix products: 20.6 us -> 8.83 us  [the longest x1 5.96 us: per_device(): updates = jnp.dot(hot, pieces, precision=lax.Precision.HIGHEST)]
    broadcast_in_dim x3 -> x0, local copies, waits for them, and re-layouts: 10.2 us -> none  [the longest x1 5.93 us: per_device(): jnp.zeros((slot_count, left_depth, block_width, block_width), jnp.bfloat16)]
  transfers between devices with their start and end apart: 5 -> 3, of which waited for: 4 -> 2; matrix products, arithmetic and copies ran while one was open for 4% -> 0% of each run, Pallas kernels for 0% -> 0%
where the time goes in v1:
time: 404 us; the launch traced here: 401 us
  waiting for transfers between devices  293 us (73%)
  blocking collectives  49.2 us (12%)
  between operations  22.2 us (5%)
  local copies, waits for them, and re-layouts  18.9 us (5%)
  matrix products  8.83 us (2%)
  starting transfers between devices  7.85 us (2%)
    reduce_scatter x1, waiting for transfers between devices, per_device(): reduced = lax.psum_scatter(updates, 'tile', scatter_dimension=0, tiled=True)  217 us
    all_gather x1, waiting for transfers between devices, per_device(): gathered = lax.all_gather(panel, 'tile', axis=0, tiled=True)  75.9 us
    unnamed x1, blocking collectives  49.2 us
  transfers between devices with their start and end apart: 3, of which 2 were waited for; matrix products, arithmetic and copies ran while one was open for 0% of the time, Pallas kernels for 0%

profile of v1, /device:TPU:1, one launch (start us, length us, event | category | flops | bytes accessed | tf_op | source)
XLA Modules:
  0.0 401.4 jit_solution(13344842714311315893)
XLA Ops:
  7.2 0.0 copy-start
  7.2 1.6 copy-done
  8.8 1.9 fusion.2
  10.7 2.3 copy.27
  13.0 0.0 copy-start.7
  13.0 0.0 copy-start.5
  13.0 0.0 copy-start.6
  13.0 7.8 %all-to-all-start = ((f32[8,8,2,32,256]{4,3,2,1,0:T(8,128)}), f32[8,8,2,32,256]{4,3,2,1,0:T(8,128)}, u32[]{:S(2)}, u32[]{:S(2)}) async-start(f32[8,8,2,32,256]{4,3,2,1,0:T(8,128)} %bitcast.45), calls=%async_computation | async-start | bytes 8388608 | tf_op jit(solution)/shard_map/to_row_owners/all_to_all | solution.py:28
  20.8 0.0 reduce-scatter.2.cloned.1.call-start
  20.8 0.0 copy-done.7
  20.8 0.6 dynamic-slice
  22.0 0.0 copy-done.5
  22.1 0.0 copy-done.6
  22.1 0.1 fusion.12
  22.2 49.2 %all-reduce = s32[64]{0:T(128)S(1)} all-reduce(s32[64]{0:T(128)S(1)} %fusion.12), channel_id=1, replica_groups=mesh['forest'=8,'tile'=32] {'forest'}, use_global_device_ids=true, to_apply=%add | all-reduce | flops 64 | bytes 512
  71.3 0.0 all-to-all-done
  71.3 5.0 %reshape.16 = f32[64,16384]{1,0:T(8,128)} reshape(f32[8,8,2,32,256]{4,3,2,1,0:T(8,128)} %all-to-all-done) | data formatting | bytes 8388608 | tf_op jit(solution)/shard_map/sum_by_group/reshape | solution.py:30
  76.3 3.4 copy.23
  79.7 6.0 %fusion = f32[64,2,32,256]{3,0,2,1:T(8,128)S(1)} fusion(f32[2,32,256,64]{2,1,0,3:T(8,128)S(1)} %bitcast.46, s32[64]{0:T(128)S(1)} %all-reduce), kind=kOutput, calls=%fused_computation | convolution fusion | flops 805314560 | bytes 8388864 | tf_op jit(solution)/shard_map/sum_by_group/dot_general | solution.py:34
  85.7 4.4 %copy.19 = f32[64,2,32,256]{3,2,1,0:T(8,128)} copy(f32[64,2,32,256]{3,0,2,1:T(8,128)S(1)} %fusion) | data formatting | bytes 8388608 | tf_op jit(solution)/shard_map/sum_by_group/dot_general | solution.py:34
  90.1 0.0 copy-start.3
  90.1 0.0 copy-start.2
  90.1 0.0 copy-start.4
  90.1 0.0 reduce-scatter.2.cloned.1.call-update
  90.1 0.0 all-gather.2.cloned.1.call-start
  90.2 216.7 %reduce-scatter.2.cloned.1.call-done = f32[2,2,32,256]{3,2,1,0:T(8,128)} async-done(((f32[64,2,32,256]{3,2,1,0:T(8,128)}), f32[2,2,32,256]{3,2,1,0:T(8,128)}) %reduce-scatter.2.cloned.1.call-update) | async-done | bytes 131088 | tf_op jit(solution)/shard_map/sum_by_group/reduce_scatter | solution.py:36
  306.9 0.0 copy-done.3
  306.9 0.9 sub.3
  307.8 0.0 copy-done.2
  307.8 0.0 copy-start.1
  307.8 0.9 fusion.5
  308.8 0.0 all-gather.2.cloned.1.call-update
  308.8 0.0 copy-done.4
  308.8 0.7 fusion.15
  317.0 75.9 %all-gather.2.cloned.1.call-done = f32[64,2,32,256]{3,2,1,0:T(8,128)} async-done(((f32[2,2,32,256]{3,2,1,0:T(8,128)}), f32[64,2,32,256]{3,2,1,0:T(8,128)}) %all-gather.2.cloned.1.call-update) | async-done | bytes 4194320 | tf_op jit(solution)/shard_map/reads/all_gather | solution.py:43
  392.9 1.0 constant_dynamic-slice_fusion.3
  393.9 0.7 pad_maximum_fusion
  394.6 0.0 copy-done.1
  (1 shorter events, 0.0 us)
Async XLA Ops:
  7.2 1.6 copy-start
  13.0 7.8 %copy-start.7 = (u32[256]{0:T(256)S(1)}, u32[256]{0:T(256)}, u32[]{:S(2)}) copy-start(u32[256]{0:T(256)} %constant.45) | copy-start | bytes 3076
  13.0 9.1 %copy-start.5 = (s32[1,8]{1,0:T(1,128)S(1)}, s32[1,8]{1,0:T(1,128)}, u32[]{:S(2)}) copy-start(s32[1,8]{1,0:T(1,128)} %param.10) | copy-start | bytes 100
  13.0 9.1 %copy-start.6 = (s32[1,8,1]{1,2,0:T(1,128)S(1)}, s32[1,8,1]{1,2,0:T(1,128)}, u32[]{:S(2)}) copy-start(s32[1,8,1]{1,2,0:T(1,128)} %param.9) | copy-start | bytes 100
  13.0 58.3 %all-to-all-start = ((f32[8,8,2,32,256]{4,3,2,1,0:T(8,128)}), f32[8,8,2,32,256]{4,3,2,1,0:T(8,128)}, u32[]{:S(2)}, u32[]{:S(2)}) async-start(f32[8,8,2,32,256]{4,3,2,1,0:T(8,128)} %bitcast.45), calls=%async_computation | async-start | bytes 8388608 | tf_op jit(solution)/shard_map/to_row_owners/all_to_all | solution.py:28
  20.8 286.1 %reduce-scatter.2.cloned.1.call-start = ((), (), s32[]{:S(2)}) async-start(), calls=%async_computation.2 | async-start | bytes 4325376 | tf_op jit(solution)/shard_map/sum_by_group/reduce_scatter | solution.py:36
  90.1 216.8 %copy-start.3 = (f32[2,2,32,256]{3,2,1,0:T(8,128)S(1)}, f32[2,2,32,256]{3,2,1,0:T(8,128)}, u32[]{:S(2)}) copy-start(f32[2,2,32,256]{3,2,1,0:T(8,128)} %param.11) | copy-start | bytes 393220
  90.1 217.7 %copy-start.2 = (f32[256,256]{1,0:T(8,128)S(1)}, f32[256,256]{1,0:T(8,128)}, u32[]{:S(2)}) copy-start(f32[256,256]{1,0:T(8,128)} %param.12) | copy-start | bytes 786436
  90.1 218.7 %copy-start.4 = (s32[128]{0:T(128)S(1)}, s32[128]{0:T(128)}, u32[]{:S(2)}) copy-start(s32[128]{0:T(128)} %param.13) | copy-start | bytes 1540
  90.1 302.8 %all-gather.2.cloned.1.call-start = ((), (), s32[]{:S(2)}) async-start(), calls=%async_computation.3 | async-start | bytes 4325376 | tf_op jit(solution)/shard_map/reads/all_gather | solution.py:43
  307.8 86.8 %copy-start.1 = (f32[2,2,32,256]{3,2,1,0:T(8,128)}, f32[2,2,32,256]{3,2,1,0:T(8,128)S(1)}, u32[]{:S(2)}) copy-start(f32[2,2,32,256]{3,2,1,0:T(8,128)S(1)} %sub.3) | copy-start | bytes 393220
Sparse Core Ops, SparseCore 0:
  90.2 216.5 reduce-scatter.1
  310.4 82.4 all-gather.1

commit v2 on v1

v2 whole, which is shorter than its diff:
```python
import functools

import jax
import jax.numpy as jnp
from jax import lax
from jax.experimental import pallas as pl
from jax.experimental.pallas import tpu as pltpu
from jax.sharding import PartitionSpec as P

MESH = pl.DeviceIdType.MESH
Y = 4
Z = 8
F = 8
CHUNKS = 2
TOP = 32767.0


def encode(v):
    most = jnp.maximum(jnp.max(jnp.abs(v), axis=0, keepdims=True), 1e-30)
    q = jnp.round(v * (TOP / most)).astype(jnp.int32).astype(jnp.int16)
    return q, most * (1.0 / TOP)


def decode(q, scale):
    return q.astype(jnp.int32).astype(jnp.float32) * scale


def kernel(owner, slot, reads, left, right, frontal, inverse, ancestor, picked, *scratch):
    (ids, meta_v, meta, x_out, xs_out, x_in, xs_in, y_out, ys_out, y_in, ys_in,
     z_out, zs_out, z_in, zs_in, total, r_out, rs_out, *rest) = scratch
    sums, rest = rest[:CHUNKS], rest[CHUNKS:]
    g_all, rest = rest[:CHUNKS], rest[CHUNKS:]
    gs_all, rest = rest[:CHUNKS], rest[CHUNKS:]
    r_all, rest = rest[:CHUNKS], rest[CHUNKS:]
    rs_all, rest = rest[:CHUNKS], rest[CHUNKS:]
    id_sem, x_sem, y_sem, z_sem, g_sem, r_sem, own_sem, meta_sem = rest

    pairs, depth, width = left.shape[:3]
    rows = width // F
    part = depth * rows // CHUNKS
    cuts = rows // part
    per_dev = frontal.shape[0]
    listed = picked.shape[0]
    f = lax.axis_index("forest")
    t = lax.axis_index("tile")
    z, y = t // Y, t % Y

    forest_peers = [((f + i) % F, t) for i in range(1, F)]
    y_peers = [(f, z * Y + (y + i) % Y) for i in range(1, Y)]
    z_peers = [(f, (z + i) % Z * Y + y) for i in range(1, Z)]
    barrier = pltpu.get_barrier_semaphore()
    for peer in forest_peers + y_peers + z_peers:
        pl.semaphore_signal(barrier, inc=1, device_id=peer, device_id_type=MESH)

    def send(src, dst, sems, at, peer):
        copy = pltpu.make_async_remote_copy(
            src_ref=src, dst_ref=dst, send_sem=sems.at[(0,) + at], recv_sem=sems.at[(1,) + at],
            device_id=peer, device_id_type=MESH,
        )
        copy.start()
        return copy

    lane = lax.broadcasted_iota(jnp.int32, (8, 128), 1)
    sub = lax.broadcasted_iota(jnp.int32, (8, 128), 0)
    down = jnp.zeros((8, 128), jnp.int32)
    along = jnp.zeros((8, 128), jnp.int32)
    for k in range(pairs):
        group = owner[k] * per_dev + slot[k]
        down = jnp.where(sub == k, group, down)
        along = jnp.where(lane == f * pairs + k, group, along)
    ids[f, 0:8, :] = down
    ids[f, 8:16, :] = along

    def products(c):
        tile, cut = c // cuts, c % cuts

        def body(k, carry):
            a = left[k, tile].reshape(F, rows, width)[:, cut * part:(cut + 1) * part]
            out = jnp.dot(
                a.reshape(F * part, width), right[k, 0], preferred_element_type=jnp.float32
            )
            for d in range(F):
                q, s = encode(out[d * part:(d + 1) * part])
                x_out[d, c, k] = q
                xs_out[d, c, k] = s
            return carry

        lax.fori_loop(0, pairs, body, 0)

    sent = []
    x_copies = {}
    for c in range(CHUNKS):
        products(c)
        if c == 0:
            pl.semaphore_wait(barrier, len(forest_peers + y_peers + z_peers))
            id_copies = [
                send(ids.at[f], ids.at[f], id_sem, (i,), peer)
                for i, peer in enumerate(forest_peers)
            ]
            sent += id_copies
        x_copies[c] = []
        for i, peer in enumerate(forest_peers):
            d = peer[0]
            x_copies[c].append(send(x_out.at[d, c], x_in.at[f, c], x_sem, (0, c, i), peer))
            x_copies[c].append(send(xs_out.at[d, c], xs_in.at[f, c], x_sem, (1, c, i), peer))
        sent += x_copies[c]
        own = [
            pltpu.make_async_copy(x_out.at[f, c], x_in.at[f, c], own_sem.at[0]),
            pltpu.make_async_copy(xs_out.at[f, c], xs_in.at[f, c], own_sem.at[1]),
        ]
        for copy in own:
            copy.start()
        for copy in own:
            copy.wait()

    for copy in id_copies:
        copy.wait_recv()
    count = F * pairs
    cols = ids[:, 0:8, :].reshape(count, 128)
    line = jnp.sum(ids[:, 8:16, :], axis=0)
    line = jnp.broadcast_to(line[None], (F, 8, 128)).reshape(count, 128)
    number = lax.broadcasted_iota(jnp.int32, (count, 128), 0)
    place = lax.broadcasted_iota(jnp.int32, (count, 128), 1)

    def latest(mask):
        at = jnp.max(jnp.where(mask, number, -1), axis=0, keepdims=True)
        return jnp.broadcast_to(jnp.where(at < 0, count, at), (8, 128))

    meta_v[0:8, :] = latest((cols == line) & (number < place))
    meta_v[8:16, :] = latest(cols == place)
    copy = pltpu.make_async_copy(meta_v, meta, meta_sem)
    copy.start()
    copy.wait()

    y_copies = {}
    for c in range(CHUNKS):
        for copy in x_copies[c]:
            copy.wait_recv()
        held = sums[c]
        held[count] = jnp.zeros((part, width), jnp.float32)

        def chain(j, carry, c=c, held=held):
            v = decode(x_in[j // pairs, c, j % pairs], xs_in[j // pairs, c, j % pairs])
            held[j] = v + held[meta[0, j]]
            return carry

        lax.fori_loop(0, count, chain, 0)
        y_copies[c] = []
        for i, peer in enumerate(y_peers):
            to = (y + i + 1) % Y

            def pack(m, carry, c=c, held=held, i=i, to=to):
                g = (m // per_dev * Y + to) * per_dev + m % per_dev
                q, s = encode(held[meta[8, g]])
                y_out[i, c, m] = q
                ys_out[i, c, m] = s
                return carry

            lax.fori_loop(0, Z * per_dev, pack, 0)
            y_copies[c].append(send(y_out.at[i, c], y_in.at[i, c], y_sem, (0, c, i), peer))
            y_copies[c].append(send(ys_out.at[i, c], ys_in.at[i, c], y_sem, (1, c, i), peer))
        sent += y_copies[c]

    z_copies = {}
    for c in range(CHUNKS):
        for copy in y_copies[c]:
            copy.wait_recv()
        held = sums[c]

        def merge(m, carry, c=c, held=held):
            g = (m // per_dev * Y + y) * per_dev + m % per_dev
            v = held[meta[8, g]]
            for i in range(Y - 1):
                v = v + decode(y_in[i, c, m], ys_in[i, c, m])
            total[c, m] = v
            q, s = encode(v)
            z_out[m // per_dev, c, m % per_dev] = q
            zs_out[m // per_dev, c, m % per_dev] = s
            return carry

        lax.fori_loop(0, Z * per_dev, merge, 0)
        z_copies[c] = []
        for i, peer in enumerate(z_peers):
            to = (z + i + 1) % Z
            z_copies[c].append(send(z_out.at[to, c], z_in.at[i, c], z_sem, (0, c, i), peer))
            z_copies[c].append(send(zs_out.at[to, c], zs_in.at[i, c], z_sem, (1, c, i), peer))
        sent += z_copies[c]

    g_copies = {}
    for c in range(CHUNKS):
        tile, cut = c // cuts, c % cuts
        for copy in z_copies[c]:
            copy.wait_recv()
        for s in range(per_dev):
            v = total[c, z * per_dev + s]
            for i in range(Z - 1):
                v = v + decode(z_in[i, c, s], zs_in[i, c, s])
            v = frontal[s, tile, cut * part:(cut + 1) * part] - v * (1.0 / depth)
            ancestor[s, tile, cut * part:(cut + 1) * part] = v
            solved = jnp.dot(
                v, inverse[...], precision=lax.Precision.HIGHEST,
                preferred_element_type=jnp.float32,
            )
            q, scale = encode(solved)
            g_all[c][z, s] = q
            gs_all[c][z, s] = scale
        g_copies[c] = []
        for i, peer in enumerate(z_peers):
            g_copies[c].append(send(g_all[c].at[z], g_all[c].at[z], g_sem, (0, c, i), peer))
            g_copies[c].append(send(gs_all[c].at[z], gs_all[c].at[z], g_sem, (1, c, i), peer))
        sent += g_copies[c]

    r_copies = {}
    for c in range(CHUNKS):
        for copy in g_copies[c]:
            copy.wait_recv()
        r_copies[c] = []
        for i in range(Y):
            to = (y + i) % Y
            for r in range(listed):
                g = reads[(z * Y + to) * listed + r]
                q = g_all[c][g // (Y * per_dev), g % per_dev]
                scale = gs_all[c][g // (Y * per_dev), g % per_dev]
                if i == 0:
                    r_all[c][y, r] = q
                    rs_all[c][y, r] = scale
                else:
                    r_out[i - 1, c, r] = q
                    rs_out[i - 1, c, r] = scale
            if i:
                peer = y_peers[i - 1]
                r_copies[c].append(
                    send(r_out.at[i - 1, c], r_all[c].at[y], r_sem, (0, c, i - 1), peer)
                )
                r_copies[c].append(
                    send(rs_out.at[i - 1, c], rs_all[c].at[y], r_sem, (1, c, i - 1), peer)
                )
        sent += r_copies[c]

    for c in range(CHUNKS):
        tile, cut = c // cuts, c % cuts
        for copy in r_copies[c]:
            copy.wait_recv()
        for r in range(listed):
            at = reads[t * listed + r] // per_dev % Y
            picked[r, tile, cut * part:(cut + 1) * part] = decode(r_all[c][at, r], rs_all[c][at, r])

    for copy in sent:
        copy.wait_send()


def per_device(
    left_panels, right_panels, dest_owner, tile_slot, frontal_tiles, diag_inverse, reader_tile
):
    left = left_panels[0]
    right = right_panels[0]
    pairs, depth, width = left.shape[:3]
    per_dev = frontal_tiles.shape[0]
    tiles = lax.axis_size("tile")
    listed = reader_tile.shape[0] // tiles
    part = depth * (width // F) // CHUNKS
    count = F * pairs
    mine = Z * per_dev

    def block(*lead):
        return [
            pltpu.VMEM(lead + (part, width), jnp.int16),
            pltpu.VMEM(lead + (1, width), jnp.float32),
        ]

    n = CHUNKS
    scratch = [
        pltpu.VMEM((F, 16, 128), jnp.int32),
        pltpu.VMEM((16, 128), jnp.int32),
        pltpu.SMEM((16, 128), jnp.int32),
        *block(F, n, pairs),
        *block(F, n, pairs),
        *block(Y - 1, n, mine),
        *block(Y - 1, n, mine),
        *block(Z, n, per_dev),
        *block(Z - 1, n, per_dev),
        pltpu.VMEM((n, mine, part, width), jnp.float32),
        *block(Y - 1, n, listed),
        *[pltpu.VMEM((count + 1, part, width), jnp.float32)] * n,
        *[block(Z, per_dev)[0]] * n,
        *[block(Z, per_dev)[1]] * n,
        *[block(Y, listed)[0]] * n,
        *[block(Y, listed)[1]] * n,
        pltpu.SemaphoreType.DMA((2, F - 1)),
        pltpu.SemaphoreType.DMA((2, 2, n, F - 1)),
        pltpu.SemaphoreType.DMA((2, 2, n, Y - 1)),
        pltpu.SemaphoreType.DMA((2, 2, n, Z - 1)),
        pltpu.SemaphoreType.DMA((2, 2, n, Z - 1)),
        pltpu.SemaphoreType.DMA((2, 2, n, Y - 1)),
        pltpu.SemaphoreType.DMA((2,)),
        pltpu.SemaphoreType.DMA,
    ]
    smem = pl.BlockSpec(memory_space=pltpu.SMEM)
    vmem = pl.BlockSpec(memory_space=pltpu.VMEM)
    return pl.pallas_call(
        kernel,
        out_shape=(
            jax.ShapeDtypeStruct(frontal_tiles.shape, jnp.float32),
            jax.ShapeDtypeStruct((listed,) + frontal_tiles.shape[1:], jnp.float32),
        ),
        in_specs=[smem, smem, smem, vmem, vmem, vmem, vmem],
        out_specs=(vmem, vmem),
        scratch_shapes=scratch,
        compiler_params=pltpu.CompilerParams(
            collective_id=0, has_side_effects=True, vmem_limit_bytes=48 << 20
        ),
        cost_estimate=pl.CostEstimate(
            flops=2 * pairs * depth * width**3, bytes_accessed=4 << 20, transcendentals=0
        ),
        name="schur_update",
    )(dest_owner[0, :, 0], tile_slot[0], reader_tile, left, right, frontal_tiles, diag_inverse)


def solution(mesh):
    placed = (
        P("forest", "tile", None, None, None),
        P("forest", "tile", None, None, None),
        P("forest", "tile", None),
        P("forest", "tile"),
        P("tile", None, "forest", None),
        P(),
        P(),
    )
    return jax.shard_map(
        per_device,
        mesh=mesh,
        in_specs=placed,
        out_specs=(P("tile", None, "forest", None), P("tile", None, "forest", None)),
        check_vma=False,
    )
```

time: 404 us -> 90.3 us (0.22)
  waiting for transfers between devices: 293 us -> 0 us
  Pallas kernels: 0 us -> 81.5 us
  blocking collectives: 49.2 us -> 0 us
  between operations: 22.2 us -> 0.66 us
  local copies, waits for them, and re-layouts: 18.9 us -> 7.99 us
  matrix products: 8.83 us -> 0 us
  starting transfers between devices: 7.85 us -> 0 us
    reduce_scatter x1 -> x0, waiting for transfers between devices: 217 us -> none  [per_device(): reduced = lax.psum_scatter(updates, 'tile', scatter_dimension=0, tiled=True)]
    pallas_call x0 -> x1, Pallas kernels: none -> 81.5 us  [per_device(): pl.pallas_call(kernel, out_shape=(jax.ShapeDtypeStruct(frontal_tiles.shap...]
    all_gather x1 -> x0, waiting for transfers between devices: 75.9 us -> none  [per_device(): gathered = lax.all_gather(panel, 'tile', axis=0, tiled=True)]
    unnamed x1 -> x0, blocking collectives: 49.2 us -> none
    dot_general x3 -> x0, matrix products: 8.83 us -> none  [the longest x1 5.96 us: per_device(): updates = jnp.dot(hot, pieces, precision=lax.Precision.HIGHEST)]
    all_to_all x1 -> x0, starting transfers between devices: 7.8 us -> none  [per_device(): lax.all_to_all(products, 'forest', split_axis=0, concat_axis=0, tiled=True)]
    reshape x2 -> x0, local copies, waits for them, and re-layouts: 7.25 us -> none  [the longest x1 4.96 us: per_device(): pieces = pieces.reshape(forest_count * pairs, depth * rows * width)]
    dot_general x1 -> x0, local copies, waits for them, and re-layouts: 4.38 us -> none  [per_device(): updates = jnp.dot(hot, pieces, precision=lax.Precision.HIGHEST)]
  transfers between devices with their start and end apart: 3 -> 0, of which waited for: 2 -> 0; matrix products, arithmetic and copies ran while one was open for 0% -> 0% of each run, Pallas kernels for 0% -> 0%
where the time goes in v2:
time: 90.3 us; the launch traced here: 90.1 us
  Pallas kernels  81.5 us (90%)
  local copies, waits for them, and re-layouts  7.99 us (9%)
    pallas_call x1, Pallas kernels, per_device(): pl.pallas_call(kernel, out_shape=(jax.ShapeDtypeStruct(frontal_tiles.shap...  81.5 us
    unnamed x16, local copies, waits for them, and re-layouts  7.99 us

profile of v2, /device:TPU:1, one launch (start us, length us, event | category | flops | bytes accessed | tf_op | source)
XLA Modules:
  0.0 90.1 jit_solution(8954425367268138970)
XLA Ops:
  0.6 0.0 copy-start
  0.6 1.6 %copy-done = bf16[1,8,2,256,256]{4,3,2,1,0:T(8,128)(2,1)S(1)} copy-done((bf16[1,8,2,256,256]{4,3,2,1,0:T(8,128)(2,1)S(1)}, bf16[1,8,2,256,256]{4,3,2,1,0:T(8,128)(2,1)}, u32[]{:S(2)}) %copy-start) | copy-done | bytes 2097176
  2.2 0.0 copy-start.1
  2.2 1.2 %copy-done.1 = bf16[1,8,1,256,256]{4,3,2,1,0:T(8,128)(2,1)S(1)} copy-done((bf16[1,8,1,256,256]{4,3,2,1,0:T(8,128)(2,1)S(1)}, bf16[1,8,1,256,256]{4,3,2,1,0:T(8,128)(2,1)}, u32[]{:S(2)}) %copy-start.1) | copy-done | bytes 1048600
  3.4 0.0 copy-start.2
  3.5 0.9 %copy-done.2 = f32[256,256]{1,0:T(8,128)S(1)} copy-done((f32[256,256]{1,0:T(8,128)S(1)}, f32[256,256]{1,0:T(8,128)}, u32[]{:S(2)}) %copy-start.2) | copy-done | bytes 262168
  4.4 0.0 copy-start.3
  4.4 0.9 %copy-done.3 = f32[2,2,32,256]{3,2,1,0:T(8,128)S(1)} copy-done((f32[2,2,32,256]{3,2,1,0:T(8,128)S(1)}, f32[2,2,32,256]{3,2,1,0:T(8,128)}, u32[]{:S(2)}) %copy-start.3) | copy-done | bytes 131096
  5.3 0.0 copy-start.4
  5.3 0.7 copy-done.4
  6.0 0.0 copy-start.5
  6.0 0.7 copy-done.5
  6.6 0.0 copy-start.6
  6.6 0.7 copy-done.6
  7.3 81.5 %schur_update.1 = (f32[2,2,32,256]{3,2,1,0:T(8,128)S(1)}, f32[4,2,32,256]{3,2,1,0:T(8,128)S(1)}) custom-call(s32[8]{0:T(128)S(1)} %bitcast.6, s32[8]{0:T(128)S(1)} %bitcast.7, s32[128]{0:T(128)S(1)} %copy-done.6, bf16[8,2,256,256]{3,2,1,0:T(8,128)(2,1)S(1)} %bitcast.4, bf16[8,1,256,256]{3,2,1,0:T(8,128)(2,1)S(1)} %bitcast.5, ...), custom_call_target="tpu_custom_call" | custom-call | flops 536870912 | bytes 4194304 | tf_op jit(solution)/shard_map/schur_update/pallas_call | solution.py:300
  88.7 0.7 copy.11
  89.4 0.7 copy.12
Async XLA Ops:
  0.6 1.6 %copy-start = (bf16[1,8,2,256,256]{4,3,2,1,0:T(8,128)(2,1)S(1)}, bf16[1,8,2,256,256]{4,3,2,1,0:T(8,128)(2,1)}, u32[]{:S(2)}) copy-start(bf16[1,8,2,256,256]{4,3,2,1,0:T(8,128)(2,1)} %param.7) | copy-start | bytes 6291460
  2.2 1.2 %copy-start.1 = (bf16[1,8,1,256,256]{4,3,2,1,0:T(8,128)(2,1)S(1)}, bf16[1,8,1,256,256]{4,3,2,1,0:T(8,128)(2,1)}, u32[]{:S(2)}) copy-start(bf16[1,8,1,256,256]{4,3,2,1,0:T(8,128)(2,1)} %param.8) | copy-start | bytes 3145732
  3.4 0.9 %copy-start.2 = (f32[256,256]{1,0:T(8,128)S(1)}, f32[256,256]{1,0:T(8,128)}, u32[]{:S(2)}) copy-start(f32[256,256]{1,0:T(8,128)} %inverse.1) | copy-start | bytes 786436
  4.4 0.9 %copy-start.3 = (f32[2,2,32,256]{3,2,1,0:T(8,128)S(1)}, f32[2,2,32,256]{3,2,1,0:T(8,128)}, u32[]{:S(2)}) copy-start(f32[2,2,32,256]{3,2,1,0:T(8,128)} %frontal.1) | copy-start | bytes 393220
  5.3 0.7 copy-start.4
  6.0 0.7 copy-start.5
  6.6 0.7 copy-start.6

commit v3 on v1

v3 whole, which is shorter than its diff:
```python
import functools

import jax
import jax.numpy as jnp
from jax import lax
from jax.experimental import pallas as pl
from jax.experimental.pallas import tpu as pltpu
from jax.sharding import PartitionSpec as P

MESH = pl.DeviceIdType.MESH
Y = 4
Z = 8
F = 8
HALF = 128
CUTS = 1
CHUNKS = 2 * CUTS
TOP = 32767.0


def scale_of(v):
    v = jnp.abs(v)
    most = functools.reduce(jnp.maximum, [v[i:i + 8] for i in range(0, v.shape[0], 8)])
    most = jnp.maximum(jnp.max(most, axis=0, keepdims=True), 1e-30)
    return most * (1.0 / TOP), TOP / most


def encode(v):
    step, back = scale_of(v)
    return jnp.round(v * back).astype(jnp.int32).astype(jnp.int16), step


def decode(q, step):
    return q.astype(jnp.int32).astype(jnp.float32) * step


def kernel(
    owner_at, slot_at, reads_at, left_at, right_at, frontal_at, inverse_at, ancestor, picked, *scratch
):
    (owner, slot, reads, left, right, frontal, inverse, product, ids, meta_v, meta,
     front, parts, parts_in, solid, x_out, xs_out, x_in, xs_in, mine, z_out, zs_out, z_in, zs_in,
     r_out, rs_out, r_in, rs_in, *rest) = scratch
    sums, rest = rest[:Y], rest[Y:]
    g_all, rest = rest[:CHUNKS], rest[CHUNKS:]
    gs_all, rest = rest[:CHUNKS], rest[CHUNKS:]
    id_sem, x_sem, z_sem, g_sem, r_sem, f_sem, a_sem, own_sem, meta_sem, in_sem = rest

    loads = [
        pltpu.make_async_copy(src, dst, in_sem.at[i])
        for i, (src, dst) in enumerate([
            (left_at, left), (right_at, right), (owner_at, owner), (slot_at, slot),
            (reads_at, reads), (frontal_at, frontal), (inverse_at, inverse),
        ])
    ]
    for copy in loads:
        copy.start()

    pairs, depth, width = left.shape[:3]
    per_dev = frontal.shape[0]
    listed = picked.shape[0]
    part = frontal.shape[2]
    rows = part // CUTS
    count = F * pairs
    around = Y * per_dev
    f = lax.axis_index("forest")
    t = lax.axis_index("tile")
    z, y = t // Y, t % Y

    x_peers = [
        ((f + i) % F, z * Y + (y + l) % Y) for l in range(Y) for i in range(F) if i or l
    ]
    y_peers = [(f, z * Y + (y + i) % Y) for i in range(1, Y)]
    z_peers = [(f, (z + i) % Z * Y + y) for i in range(1, Z)]
    barrier = pltpu.get_barrier_semaphore()
    for peer in x_peers + z_peers:
        pl.semaphore_signal(barrier, inc=1, device_id=peer, device_id_type=MESH)

    def send(src, dst, sems, at, peer):
        copy = pltpu.make_async_remote_copy(
            src_ref=src, dst_ref=dst, send_sem=sems.at[(0,) + at], recv_sem=sems.at[(1,) + at],
            device_id=peer, device_id_type=MESH,
        )
        copy.start()
        return copy

    loads[2].wait()
    loads[3].wait()
    lane = lax.broadcasted_iota(jnp.int32, (8, 128), 1)
    sub = lax.broadcasted_iota(jnp.int32, (8, 128), 0)
    down = jnp.zeros((8, 128), jnp.int32)
    along = jnp.zeros((8, 128), jnp.int32)
    for k in range(pairs):
        group = owner[k] * per_dev + slot[k]
        down = jnp.where(sub == k, group, down)
        along = jnp.where(lane == f * pairs + k, group, along)
    ids[y, f, 0:8, :] = down
    ids[y, f, 8:16, :] = along

    def block_of(ff, yy):
        return yy // 2 * (2 * F) + ff * 2 + yy % 2

    def multiply(col):
        def body(k, carry):
            b = right[k, 0, :, col * HALF:(col + 1) * HALF]
            for tile in range(depth):
                product[col, k, tile * width:(tile + 1) * width] = jnp.dot(
                    left[k, tile], b, preferred_element_type=jnp.float32
                )
            return carry

        lax.fori_loop(0, pairs, body, 0)

    sent = []
    x_copies, z_copies, g_copies, r_copies = {}, {}, {}, {}
    owns = {}

    def start_x(c):
        cut, col = c // 2, c % 2
        if cut == 0:
            multiply(col)

        def pack(b, carry):
            at = pl.multiple_of(b * part + cut * rows, 8)
            v = jnp.concatenate(
                [product[col, k, pl.ds(at, rows)] for k in range(pairs)], axis=0
            )
            x_out[b, c], xs_out[b, c] = encode(v)
            return carry

        lax.fori_loop(0, F * Y, pack, 0, unroll=4)
        if c == 0:
            pl.semaphore_wait(barrier, len(x_peers + z_peers))
        x_copies[c] = []
        for i, peer in enumerate(x_peers):
            b = block_of(peer[0], peer[1] % Y)
            x_copies[c] += [
                send(x_out.at[b, c], x_in.at[y, f, c], x_sem, (0, c, i), peer),
                send(xs_out.at[b, c], xs_in.at[y, f, c], x_sem, (1, c, i), peer),
            ]
        sent.extend(x_copies[c])
        b = block_of(f, y)
        owns[c] = [
            pltpu.make_async_copy(x_out.at[b, c], x_in.at[y, f, c], own_sem.at[0, c]),
            pltpu.make_async_copy(xs_out.at[b, c], xs_in.at[y, f, c], own_sem.at[1, c]),
        ]
        for copy in owns[c]:
            copy.start()

    loads[0].wait()
    loads[1].wait()
    start_x(0)
    id_copies = [
        send(ids.at[y, f], ids.at[y, f], id_sem, (i,), peer) for i, peer in enumerate(x_peers)
    ]
    for copy in loads[4:]:
        copy.wait()
    front_copies = [
        send(frontal.at[:, peer[1] % Y], front.at[y], f_sem, (i,), peer)
        for i, peer in enumerate(y_peers)
    ]
    sent.extend(id_copies + front_copies)
    front[y] = frontal[:, y]
    for c in range(1, CHUNKS):
        start_x(c)

    for copy in id_copies:
        copy.wait_recv()
    number = lax.broadcasted_iota(jnp.int32, (count, 128), 0)
    place = lax.broadcasted_iota(jnp.int32, (count, 128), 1)

    def latest(mask):
        at = jnp.max(jnp.where(mask, number, -1), axis=0, keepdims=True)
        return jnp.broadcast_to(jnp.where(at < 0, count, at), (8, 128))

    for yy in range(Y):
        cols = ids[yy, :, 0:8, :].reshape(count, 128)
        line = jnp.sum(ids[yy, :, 8:16, :], axis=0)
        line = jnp.broadcast_to(line[None], (F, 8, 128)).reshape(count, 128)
        meta_v[yy * 16:yy * 16 + 8, :] = latest((cols == line) & (number < place))
        meta_v[yy * 16 + 8:yy * 16 + 16, :] = latest(cols == place)
        sums[yy][count] = jnp.zeros((rows, HALF), jnp.float32)
    copy = pltpu.make_async_copy(meta_v, meta, meta_sem)
    copy.start()
    copy.wait()

    def start_z(c):
        for copy in x_copies[c]:
            copy.wait_recv()
        for copy in owns[c]:
            copy.wait()

        def chain(ff, carry):
            values = [decode(x_in[yy, ff, c], xs_in[yy, ff, c]) for yy in range(Y)]
            for k in range(pairs):
                j = ff * pairs + k
                for yy in range(Y):
                    earlier = sums[yy][meta[yy * 16, j]]
                    sums[yy][j] = values[yy][k * rows:(k + 1) * rows] + earlier
            return carry

        lax.fori_loop(0, F, chain, 0, unroll=2)

        def pack(zz, carry):
            values = []
            for m in range(around):
                g = zz * around + m
                values.append(sum(sums[yy][meta[yy * 16 + 8, g]] for yy in range(Y)))
            v = jnp.concatenate(values, axis=0)
            mine[c, zz] = v
            z_out[zz, c], zs_out[zz, c] = encode(v)
            return carry

        lax.fori_loop(0, Z, pack, 0, unroll=2)
        z_copies[c] = []
        for i, peer in enumerate(z_peers):
            to = (z + i + 1) % Z
            z_copies[c] += [
                send(z_out.at[to, c], z_in.at[i, c], z_sem, (0, c, i), peer),
                send(zs_out.at[to, c], zs_in.at[i, c], z_sem, (1, c, i), peer),
            ]
        sent.extend(z_copies[c])

    def dot(a, b):
        return jnp.dot(
            a, b, precision=lax.Precision.HIGHEST, preferred_element_type=jnp.float32
        )

    a_copies = []

    def start_g(c):
        cut, col = c // 2, c % 2
        at = slice(cut * rows, (cut + 1) * rows)
        cols = slice(col * HALF, (col + 1) * HALF)
        if c == 0:
            for copy in front_copies:
                copy.wait_recv()
        for copy in z_copies[c]:
            copy.wait_recv()
        v = mine[c, z]
        for i in range(Z - 1):
            v = v + decode(z_in[i, c], zs_in[i, c])
        before = [front[m // per_dev, m % per_dev, at, cols] for m in range(around)]
        v = jnp.concatenate(before, axis=0) - v * (1.0 / depth)
        solid[c] = v
        for m in range(around):
            parts[m // per_dev, m % per_dev, at, cols] = v[m * rows:(m + 1) * rows]
        solved = dot(v, inverse[cols, cols])
        if col:
            solved = solved + dot(solid[c - 1], inverse[0:HALF, cols])
        q, step = encode(solved)
        for m in range(around * rows // 16):
            g_all[c][z, m] = q[m * 16:(m + 1) * 16]
        gs_all[c][z] = step
        g_copies[c] = []
        for i, peer in enumerate(z_peers):
            g_copies[c] += [
                send(g_all[c].at[z], g_all[c].at[z], g_sem, (0, c, i), peer),
                send(gs_all[c].at[z], gs_all[c].at[z], g_sem, (1, c, i), peer),
            ]
        sent.extend(g_copies[c])
        if c == CHUNKS - 1:
            for i, peer in enumerate(y_peers):
                a_copies.append(
                    send(parts.at[peer[1] % Y], parts_in.at[y], a_sem, (i,), peer)
                )
            sent.extend(a_copies)
            parts_in[y] = parts[y]

    def start_r(c):
        for copy in g_copies[c]:
            copy.wait_recv()
        r_copies[c] = []
        for i in range(Y):
            to = (y + i) % Y
            values = []
            for r in range(listed):
                g = reads[(z * Y + to) * listed + r]
                at = g % around
                if rows == 16:
                    q = g_all[c][g // around, at].astype(jnp.int32)
                else:
                    q = g_all[c][g // around, at // 2].astype(jnp.int32)
                    q = jnp.where(at % 2 == 1, q[8:16], q[0:8])
                values.append(q)
            q = jnp.concatenate(values, axis=0).astype(jnp.int16)
            for r in range(listed):
                g = reads[(z * Y + to) * listed + r]
                step = gs_all[c][g // around]
                if i == 0:
                    rs_in[y, c, r] = step
                else:
                    rs_out[i - 1, c, r] = step
            if i == 0:
                r_in[y, c] = q
                continue
            r_out[i - 1, c] = q
            peer = y_peers[i - 1]
            r_copies[c] += [
                send(r_out.at[i - 1, c], r_in.at[y, c], r_sem, (0, c, i - 1), peer),
                send(rs_out.at[i - 1, c], rs_in.at[y, c], r_sem, (1, c, i - 1), peer),
            ]
        sent.extend(r_copies[c])

    def finish(c):
        cut, col = c // 2, c % 2
        for copy in r_copies[c]:
            copy.wait_recv()
        for yy in range(Y):
            q = r_in[yy, c].astype(jnp.int32).astype(jnp.float32)
            for r in range(listed):
                picked[r, yy, cut * rows:(cut + 1) * rows, col * HALF:(col + 1) * HALF] = (
                    q[r * rows:(r + 1) * rows] * rs_in[yy, c, r]
                )

    stages = (start_z, start_g, start_r, finish)
    for wave in range(CHUNKS + len(stages) - 1):
        for number_of, stage in reversed(list(enumerate(stages))):
            if 0 <= wave - number_of < CHUNKS:
                stage(wave - number_of)

    for copy in a_copies:
        copy.wait_recv()
    for yy in range(Y):
        for s in range(per_dev):
            ancestor[s, yy] = parts_in[yy, s]
    for copy in sent:
        copy.wait_send()


def per_device(
    left_panels, right_panels, dest_owner, tile_slot, frontal_tiles, diag_inverse, reader_tile
):
    left = left_panels[0]
    right = right_panels[0]
    pairs, depth, width = left.shape[:3]
    per_dev = frontal_tiles.shape[0]
    listed = reader_tile.shape[0] // lax.axis_size("tile")
    part = depth * (width // F) // Y
    rows = part // CUTS
    count = F * pairs
    around = Y * per_dev
    frontal = frontal_tiles.reshape(per_dev, Y, part, width)
    n = CHUNKS

    def f32(*shape):
        return pltpu.VMEM(shape, jnp.float32)

    def i16(*shape):
        return pltpu.VMEM(shape, jnp.int16)

    dma = pltpu.SemaphoreType.DMA
    scratch = [
        pltpu.SMEM((pairs,), jnp.int32),
        pltpu.SMEM((pairs,), jnp.int32),
        pltpu.SMEM(reader_tile.shape, jnp.int32),
        pltpu.VMEM(left.shape, left.dtype),
        pltpu.VMEM(right.shape, right.dtype),
        f32(*frontal.shape),
        f32(*diag_inverse.shape),
        f32(2, pairs, depth * width, HALF),
        pltpu.VMEM((Y, F, 16, 128), jnp.int32),
        pltpu.VMEM((Y * 16, 128), jnp.int32),
        pltpu.SMEM((Y * 16, 128), jnp.int32),
        f32(Y, per_dev, part, width),
        f32(Y, per_dev, part, width),
        f32(Y, per_dev, part, width),
        f32(n, around * rows, HALF),
        i16(F * Y, n, pairs * rows, HALF),
        f32(F * Y, n, 1, HALF),
        i16(Y, F, n, pairs * rows, HALF),
        f32(Y, F, n, 1, HALF),
        f32(n, Z, around * rows, HALF),
        i16(Z, n, around * rows, HALF),
        f32(Z, n, 1, HALF),
        i16(Z - 1, n, around * rows, HALF),
        f32(Z - 1, n, 1, HALF),
        i16(Y - 1, n, listed * rows, HALF),
        f32(Y - 1, n, listed, 1, HALF),
        i16(Y, n, listed * rows, HALF),
        f32(Y, n, listed, 1, HALF),
        *[f32(count + 1, rows, HALF)] * Y,
        *[i16(Z, around * rows // 16, 16, HALF)] * n,
        *[f32(Z, 1, HALF)] * n,
        dma((2, F * Y - 1)),
        dma((2, 2, n, F * Y - 1)),
        dma((2, 2, n, Z - 1)),
        dma((2, 2, n, Z - 1)),
        dma((2, 2, n, Y - 1)),
        dma((2, Y - 1)),
        dma((2, Y - 1)),
        dma((2, n)),
        dma,
        dma((7,)),
    ]
    any_place = pl.BlockSpec(memory_space=pl.ANY)
    vmem = pl.BlockSpec(memory_space=pltpu.VMEM)
    ancestor, picked = pl.pallas_call(
        kernel,
        out_shape=(
            jax.ShapeDtypeStruct(frontal.shape, jnp.float32),
            jax.ShapeDtypeStruct((listed,) + frontal.shape[1:], jnp.float32),
        ),
        in_specs=[any_place] * 7,
        out_specs=(vmem, vmem),
        scratch_shapes=scratch,
        compiler_params=pltpu.CompilerParams(
            collective_id=0, has_side_effects=True, vmem_limit_bytes=60 << 20
        ),
        cost_estimate=pl.CostEstimate(
            flops=2 * pairs * depth * width**3, bytes_accessed=4 << 20, transcendentals=0
        ),
        name="schur_update",
    )(dest_owner[0, :, 0], tile_slot[0], reader_tile, left, right, frontal, diag_inverse)
    return (
        ancestor.reshape(frontal_tiles.shape),
        picked.reshape((listed,) + frontal_tiles.shape[1:]),
    )


def solution(mesh):
    placed = (
        P("forest", "tile", None, None, None),
        P("forest", "tile", None, None, None),
        P("forest", "tile", None),
        P("forest", "tile"),
        P("tile", None, "forest", None),
        P(),
        P(),
    )
    return jax.shard_map(
        per_device,
        mesh=mesh,
        in_specs=placed,
        out_specs=(P("tile", None, "forest", None), P("tile", None, "forest", None)),
        check_vma=False,
    )
```

time: 404 us -> 76.4 us (0.19)
  waiting for transfers between devices: 293 us -> 0 us
  Pallas kernels: 0 us -> 72.4 us
  blocking collectives: 49.2 us -> 0 us
  between operations: 22.2 us -> 0.64 us
  local copies, waits for them, and re-layouts: 18.9 us -> 3.24 us
  matrix products: 8.83 us -> 0 us
  starting transfers between devices: 7.85 us -> 0 us
    reduce_scatter x1 -> x0, waiting for transfers between devices: 217 us -> none  [per_device(): reduced = lax.psum_scatter(updates, 'tile', scatter_dimension=0, tiled=True)]
    all_gather x1 -> x0, waiting for transfers between devices: 75.9 us -> none  [per_device(): gathered = lax.all_gather(panel, 'tile', axis=0, tiled=True)]
    pallas_call x0 -> x1, Pallas kernels: none -> 72.4 us  [per_device(): pl.pallas_call(kernel, out_shape=(jax.ShapeDtypeStruct(frontal.shape, jnp...]
    unnamed x1 -> x0, blocking collectives: 49.2 us -> none
    dot_general x3 -> x0, matrix products: 8.83 us -> none  [the longest x1 5.96 us: per_device(): updates = jnp.dot(hot, pieces, precision=lax.Precision.HIGHEST)]
    all_to_all x1 -> x0, starting transfers between devices: 7.8 us -> none  [per_device(): lax.all_to_all(products, 'forest', split_axis=0, concat_axis=0, tiled=True)]
    reshape x2 -> x0, local copies, waits for them, and re-layouts: 7.25 us -> none  [the longest x1 4.96 us: per_device(): pieces = pieces.reshape(forest_count * pairs, depth * rows * width)]
    dot_general x1 -> x0, local copies, waits for them, and re-layouts: 4.38 us -> none  [per_device(): updates = jnp.dot(hot, pieces, precision=lax.Precision.HIGHEST)]
  transfers between devices with their start and end apart: 3 -> 0, of which waited for: 2 -> 0; matrix products, arithmetic and copies ran while one was open for 0% -> 0% of each run, Pallas kernels for 0% -> 0%
where the time goes in v3:
time: 76.4 us; the launch traced here: 76.2 us
  Pallas kernels  72.4 us (95%)
  local copies, waits for them, and re-layouts  3.24 us (4%)
    pallas_call x1, Pallas kernels, per_device(): pl.pallas_call(kernel, out_shape=(jax.ShapeDtypeStruct(frontal.shape, jnp...  72.4 us
    unnamed x2, local copies, waits for them, and re-layouts  3.24 us

profile of v3, /device:TPU:1, one launch (start us, length us, event | category | flops | bytes accessed | tf_op | source)
XLA Modules:
  0.0 76.2 jit_solution(17641347509504517491)
XLA Ops:
  0.6 72.4 %schur_update.1 = (f32[2,4,16,256]{3,2,1,0:T(8,128)}, f32[4,4,16,256]{3,2,1,0:T(8,128)}) custom-call(s32[8]{0:T(128)} %bitcast.12, s32[8]{0:T(128)} %bitcast.13, s32[128]{0:T(128)} %reads_at.1, bf16[8,2,256,256]{3,2,1,0:T(8,128)(2,1)} %bitcast.7, bf16[8,1,256,256]{3,2,1,0:T(8,128)(2,1)} %bitcast.8, f32[2,4,16,256]{3,2,1,0:T(8,128)} %bitcast.10, ...), custom_call_target="tpu_custom_call" | custom-call | flops 536870912 | bytes 4194304 | tf_op jit(solution)/shard_map/schur_update/pallas_call | solution.py:396
  73.0 1.6 %copy.11 = f32[2,2,32,256]{3,2,1,0:T(8,128)} copy(f32[2,2,32,256]{3,2,1,0:T(8,128)} %bitcast.11) | data formatting | bytes 262144
  74.6 1.7 %copy.12 = f32[4,2,32,256]{3,2,1,0:T(8,128)} copy(f32[4,2,32,256]{3,2,1,0:T(8,128)} %bitcast.9) | data formatting | bytes 524288

commit v4 on v3

--- a/solution.py
+++ b/solution.py
@@ -75,12 +75,13 @@
         pl.semaphore_signal(barrier, inc=1, device_id=peer, device_id_type=MESH)
 
     def send(src, dst, sems, at, peer):
-        copy = pltpu.make_async_remote_copy(
+        pltpu.make_async_remote_copy(
             src_ref=src, dst_ref=dst, send_sem=sems.at[(0,) + at], recv_sem=sems.at[(1,) + at],
             device_id=peer, device_id_type=MESH,
-        )
-        copy.start()
-        return copy
+        ).start()
+
+    def wait(way, like, sems, at):
+        pltpu.make_async_copy(like, like, sems.at[(way,) + at]).wait()
 
     loads[2].wait()
     loads[3].wait()
@@ -92,8 +93,8 @@
         group = owner[k] * per_dev + slot[k]
         down = jnp.where(sub == k, group, down)
         along = jnp.where(lane == f * pairs + k, group, along)
-    ids[y, f, 0:8, :] = down
-    ids[y, f, 8:16, :] = along
+    ids[y * F + f, 0:8, :] = down
+    ids[y * F + f, 8:16, :] = along
 
     def block_of(ff, yy):
         return yy // 2 * (2 * F) + ff * 2 + yy % 2
@@ -109,8 +110,7 @@
 
         lax.fori_loop(0, pairs, body, 0)
 
-    sent = []
-    x_copies, z_copies, g_copies, r_copies = {}, {}, {}, {}
+    last = F * Y - 1
     owns = {}
 
     def start_x(c):
@@ -129,18 +129,14 @@
         lax.fori_loop(0, F * Y, pack, 0, unroll=4)
         if c == 0:
             pl.semaphore_wait(barrier, len(x_peers + z_peers))
-        x_copies[c] = []
-        for i, peer in enumerate(x_peers):
+        for peer in x_peers:
             b = block_of(peer[0], peer[1] % Y)
-            x_copies[c] += [
-                send(x_out.at[b, c], x_in.at[y, f, c], x_sem, (0, c, i), peer),
-                send(xs_out.at[b, c], xs_in.at[y, f, c], x_sem, (1, c, i), peer),
-            ]
-        sent.extend(x_copies[c])
+            send(x_out.at[b, c], x_in.at[y * F + f, c], x_sem, (0, c), peer)
+            send(xs_out.at[b, c], xs_in.at[y * F + f, c], x_sem, (1, c), peer)
         b = block_of(f, y)
         owns[c] = [
-            pltpu.make_async_copy(x_out.at[b, c], x_in.at[y, f, c], own_sem.at[0, c]),
-            pltpu.make_async_copy(xs_out.at[b, c], xs_in.at[y, f, c], own_sem.at[1, c]),
+            pltpu.make_async_copy(x_out.at[b, c], x_in.at[y * F + f, c], own_sem.at[0, c]),
+            pltpu.make_async_copy(xs_out.at[b, c], xs_in.at[y * F + f, c], own_sem.at[1, c]),
         ]
         for copy in owns[c]:
             copy.start()
@@ -148,22 +144,17 @@
     loads[0].wait()
     loads[1].wait()
     start_x(0)
-    id_copies = [
-        send(ids.at[y, f], ids.at[y, f], id_sem, (i,), peer) for i, peer in enumerate(x_peers)
-    ]
+    for peer in x_peers:
+        send(ids.at[y * F + f], ids.at[y * F + f], id_sem, (), peer)
     for copy in loads[4:]:
         copy.wait()
-    front_copies = [
-        send(frontal.at[:, peer[1] % Y], front.at[y], f_sem, (i,), peer)
-        for i, peer in enumerate(y_peers)
-    ]
-    sent.extend(id_copies + front_copies)
+    for peer in y_peers:
+        send(frontal.at[:, peer[1] % Y], front.at[y], f_sem, (), peer)
     front[y] = frontal[:, y]
     for c in range(1, CHUNKS):
         start_x(c)
 
-    for copy in id_copies:
-        copy.wait_recv()
+    wait(1, ids.at[pl.ds(0, last)], id_sem, ())
     number = lax.broadcasted_iota(jnp.int32, (count, 128), 0)
     place = lax.broadcasted_iota(jnp.int32, (count, 128), 1)
 
@@ -172,8 +163,8 @@
         return jnp.broadcast_to(jnp.where(at < 0, count, at), (8, 128))
 
     for yy in range(Y):
-        cols = ids[yy, :, 0:8, :].reshape(count, 128)
-        line = jnp.sum(ids[yy, :, 8:16, :], axis=0)
+        cols = ids[yy * F:(yy + 1) * F, 0:8, :].reshape(count, 128)
+        line = jnp.sum(ids[yy * F:(yy + 1) * F, 8:16, :], axis=0)
         line = jnp.broadcast_to(line[None], (F, 8, 128)).reshape(count, 128)
         meta_v[yy * 16:yy * 16 + 8, :] = latest((cols == line) & (number < place))
         meta_v[yy * 16 + 8:yy * 16 + 16, :] = latest(cols == place)
@@ -183,13 +174,13 @@
     copy.wait()
 
     def start_z(c):
-        for copy in x_copies[c]:
-            copy.wait_recv()
+        wait(1, x_in.at[pl.ds(0, last), c], x_sem, (0, c))
+        wait(1, xs_in.at[pl.ds(0, last), c], x_sem, (1, c))
         for copy in owns[c]:
             copy.wait()
 
         def chain(ff, carry):
-            values = [decode(x_in[yy, ff, c], xs_in[yy, ff, c]) for yy in range(Y)]
+            values = [decode(x_in[yy * F + ff, c], xs_in[yy * F + ff, c]) for yy in range(Y)]
             for k in range(pairs):
                 j = ff * pairs + k
                 for yy in range(Y):
@@ -210,31 +201,24 @@
             return carry
 
         lax.fori_loop(0, Z, pack, 0, unroll=2)
-        z_copies[c] = []
         for i, peer in enumerate(z_peers):
             to = (z + i + 1) % Z
-            z_copies[c] += [
-                send(z_out.at[to, c], z_in.at[i, c], z_sem, (0, c, i), peer),
-                send(zs_out.at[to, c], zs_in.at[i, c], z_sem, (1, c, i), peer),
-            ]
-        sent.extend(z_copies[c])
+            send(z_out.at[to, c], z_in.at[i, c], z_sem, (0, c), peer)
+            send(zs_out.at[to, c], zs_in.at[i, c], z_sem, (1, c), peer)
 
     def dot(a, b):
         return jnp.dot(
             a, b, precision=lax.Precision.HIGHEST, preferred_element_type=jnp.float32
         )
-
-    a_copies = []
 
     def start_g(c):
         cut, col = c // 2, c % 2
         at = slice(cut * rows, (cut + 1) * rows)
         cols = slice(col * HALF, (col + 1) * HALF)
         if c == 0:
-            for copy in front_copies:
-                copy.wait_recv()
-        for copy in z_copies[c]:
-            copy.wait_recv()
+            wait(1, front.at[pl.ds(0, Y - 1)], f_sem, ())
+        wait(1, z_in.at[:, c], z_sem, (0, c))
+        wait(1, zs_in.at[:, c], z_sem, (1, c))
         v = mine[c, z]
         for i in range(Z - 1):
             v = v + decode(z_in[i, c], zs_in[i, c])
@@ -250,25 +234,17 @@
         for m in range(around * rows // 16):
             g_all[c][z, m] = q[m * 16:(m + 1) * 16]
         gs_all[c][z] = step
-        g_copies[c] = []
-        for i, peer in enumerate(z_peers):
-            g_copies[c] += [
-                send(g_all[c].at[z], g_all[c].at[z], g_sem, (0, c, i), peer),
-                send(gs_all[c].at[z], gs_all[c].at[z], g_sem, (1, c, i), peer),
-            ]
-        sent.extend(g_copies[c])
+        for peer in z_peers:
+            send(g_all[c].at[z], g_all[c].at[z], g_sem, (0, c), peer)
+            send(gs_all[c].at[z], gs_all[c].at[z], g_sem, (1, c), peer)
         if c == CHUNKS - 1:
-            for i, peer in enumerate(y_peers):
-                a_copies.append(
-                    send(parts.at[peer[1] % Y], parts_in.at[y], a_sem, (i,), peer)
-                )
-            sent.extend(a_copies)
+            for peer in y_peers:
+                send(parts.at[peer[1] % Y], parts_in.at[y], a_sem, (), peer)
             parts_in[y] = parts[y]
 
     def start_r(c):
-        for copy in g_copies[c]:
-            copy.wait_recv()
-        r_copies[c] = []
+        wait(1, g_all[c].at[pl.ds(0, Z - 1)], g_sem, (0, c))
+        wait(1, gs_all[c].at[pl.ds(0, Z - 1)], g_sem, (1, c))
         for i in range(Y):
             to = (y + i) % Y
             values = []
@@ -294,16 +270,13 @@
                 continue
             r_out[i - 1, c] = q
             peer = y_peers[i - 1]
-            r_copies[c] += [
-                send(r_out.at[i - 1, c], r_in.at[y, c], r_sem, (0, c, i - 1), peer),
-                send(rs_out.at[i - 1, c], rs_in.at[y, c], r_sem, (1, c, i - 1), peer),
-            ]
-        sent.extend(r_copies[c])
+            send(r_out.at[i - 1, c], r_in.at[y, c], r_sem, (0, c), peer)
+            send(rs_out.at[i - 1, c], rs_in.at[y, c], r_sem, (1, c), peer)
 
     def finish(c):
         cut, col = c // 2, c % 2
-        for copy in r_copies[c]:
-            copy.wait_recv()
+        wait(1, r_in.at[pl.ds(0, Y - 1), c], r_sem, (0, c))
+        wait(1, rs_in.at[pl.ds(0, Y - 1), c], r_sem, (1, c))
         for yy in range(Y):
             q = r_in[yy, c].astype(jnp.int32).astype(jnp.float32)
             for r in range(listed):
@@ -317,13 +290,22 @@
             if 0 <= wave - number_of < CHUNKS:
                 stage(wave - number_of)
 
-    for copy in a_copies:
-        copy.wait_recv()
+    wait(1, parts_in.at[pl.ds(0, Y - 1)], a_sem, ())
     for yy in range(Y):
         for s in range(per_dev):
             ancestor[s, yy] = parts_in[yy, s]
-    for copy in sent:
-        copy.wait_send()
+    wait(0, ids.at[pl.ds(0, last)], id_sem, ())
+    wait(0, front.at[pl.ds(0, Y - 1)], f_sem, ())
+    wait(0, parts.at[pl.ds(0, Y - 1)], a_sem, ())
+    for c in range(CHUNKS):
+        wait(0, x_out.at[pl.ds(0, last), c], x_sem, (0, c))
+        wait(0, xs_out.at[pl.ds(0, last), c], x_sem, (1, c))
+        wait(0, z_out.at[pl.ds(0, Z - 1), c], z_sem, (0, c))
+        wait(0, zs_out.at[pl.ds(0, Z - 1), c], z_sem, (1, c))
+        wait(0, g_all[c].at[pl.ds(0, Z - 1)], g_sem, (0, c))
+        wait(0, gs_all[c].at[pl.ds(0, Z - 1)], g_sem, (1, c))
+        wait(0, r_out.at[:, c], r_sem, (0, c))
+        wait(0, rs_out.at[:, c], r_sem, (1, c))
 
 
 def per_device(
@@ -357,7 +339,7 @@
         f32(*frontal.shape),
         f32(*diag_inverse.shape),
         f32(2, pairs, depth * width, HALF),
-        pltpu.VMEM((Y, F, 16, 128), jnp.int32),
+        pltpu.VMEM((Y * F, 16, 128), jnp.int32),
         pltpu.VMEM((Y * 16, 128), jnp.int32),
         pltpu.SMEM((Y * 16, 128), jnp.int32),
         f32(Y, per_dev, part, width),
@@ -366,8 +348,8 @@
         f32(n, around * rows, HALF),
         i16(F * Y, n, pairs * rows, HALF),
         f32(F * Y, n, 1, HALF),
-        i16(Y, F, n, pairs * rows, HALF),
-        f32(Y, F, n, 1, HALF),
+        i16(Y * F, n, pairs * rows, HALF),
+        f32(Y * F, n, 1, HALF),
         f32(n, Z, around * rows, HALF),
         i16(Z, n, around * rows, HALF),
         f32(Z, n, 1, HALF),
@@ -380,18 +362,18 @@
         *[f32(count + 1, rows, HALF)] * Y,
         *[i16(Z, around * rows // 16, 16, HALF)] * n,
         *[f32(Z, 1, HALF)] * n,
-        dma((2, F * Y - 1)),
-        dma((2, 2, n, F * Y - 1)),
-        dma((2, 2, n, Z - 1)),
-        dma((2, 2, n, Z - 1)),
-        dma((2, 2, n, Y - 1)),
-        dma((2, Y - 1)),
-        dma((2, Y - 1)),
+        dma((2,)),
+        dma((2, 2, n)),
+        dma((2, 2, n)),
+        dma((2, 2, n)),
+        dma((2, 2, n)),
+        dma((2,)),
+        dma((2,)),
         dma((2, n)),
         dma,
         dma((7,)),
     ]
-    any_place = pl.BlockSpec(memory_space=pl.ANY)
+    hbm = pl.BlockSpec(memory_space=pltpu.HBM)
     vmem = pl.BlockSpec(memory_space=pltpu.VMEM)
     ancestor, picked = pl.pallas_call(
         kernel,
@@ -399,7 +381,7 @@
             jax.ShapeDtypeStruct(frontal.shape, jnp.float32),
             jax.ShapeDtypeStruct((listed,) + frontal.shape[1:], jnp.float32),
         ),
-        in_specs=[any_place] * 7,
+        in_specs=[hbm] * 7,
         out_specs=(vmem, vmem),
         scratch_shapes=scratch,
         compiler_params=pltpu.CompilerParams(

time: 76.4 us -> 71.8 us (0.940)
  Pallas kernels: 72.4 us -> 67.7 us
    pallas_call x1, Pallas kernels: 72.4 us -> 67.7 us  [per_device(): pl.pallas_call(kernel, out_shape=(jax.ShapeDtypeStruct(frontal.shape, jnp...]
where the time goes in v4:
time: 71.8 us; the launch traced here: 71.6 us
  Pallas kernels  67.7 us (94%)
  local copies, waits for them, and re-layouts  3.24 us (5%)
    pallas_call x1, Pallas kernels, per_device(): pl.pallas_call(kernel, out_shape=(jax.ShapeDtypeStruct(frontal.shape, jnp...  67.7 us
    unnamed x2, local copies, waits for them, and re-layouts  3.24 us

profile of v4, /device:TPU:1, one launch (start us, length us, event | category | flops | bytes accessed | tf_op | source)
XLA Modules:
  0.0 71.6 jit_solution(16641025353595678249)
XLA Ops:
  0.6 67.7 %schur_update.1 = (f32[2,4,16,256]{3,2,1,0:T(8,128)}, f32[4,4,16,256]{3,2,1,0:T(8,128)}) custom-call(s32[8]{0:T(128)} %bitcast.12, s32[8]{0:T(128)} %bitcast.13, s32[128]{0:T(128)} %reads_at.1, bf16[8,2,256,256]{3,2,1,0:T(8,128)(2,1)} %bitcast.7, bf16[8,1,256,256]{3,2,1,0:T(8,128)(2,1)} %bitcast.8, f32[2,4,16,256]{3,2,1,0:T(8,128)} %bitcast.10, ...), custom_call_target="tpu_custom_call" | custom-call | flops 536870912 | bytes 4194304 | tf_op jit(solution)/shard_map/schur_update/pallas_call | solution.py:378
  68.4 1.6 %copy.11 = f32[2,2,32,256]{3,2,1,0:T(8,128)} copy(f32[2,2,32,256]{3,2,1,0:T(8,128)} %bitcast.11) | data formatting | bytes 262144
  69.9 1.7 %copy.12 = f32[4,2,32,256]{3,2,1,0:T(8,128)} copy(f32[4,2,32,256]{3,2,1,0:T(8,128)} %bitcast.9) | data formatting | bytes 524288

commit v5 on v4

--- a/solution.py
+++ b/solution.py
@@ -378,8 +378,8 @@
     ancestor, picked = pl.pallas_call(
         kernel,
         out_shape=(
-            jax.ShapeDtypeStruct(frontal.shape, jnp.float32),
-            jax.ShapeDtypeStruct((listed,) + frontal.shape[1:], jnp.float32),
+            pltpu.VMEM(frontal.shape, jnp.float32),
+            pltpu.VMEM((listed,) + frontal.shape[1:], jnp.float32),
         ),
         in_specs=[hbm] * 7,
         out_specs=(vmem, vmem),

time: 71.8 us -> 69.9 us (0.974)
  local copies, waits for them, and re-layouts: 3.24 us -> 1.36 us
    unnamed x2, local copies, waits for them, and re-layouts: 3.24 us -> 1.36 us
where the time goes in v5:
time: 69.9 us
  Pallas kernels  67.9 us (97%)
  local copies, waits for them, and re-layouts  1.36 us (2%)
    pallas_call x1, Pallas kernels, per_device(): pl.pallas_call(kernel, out_shape=(pltpu.VMEM(frontal.shape, jnp.float32),...  67.9 us

profile of v5, /device:TPU:1, one launch (start us, length us, event | category | flops | bytes accessed | tf_op | source)
XLA Modules:
  0.0 69.9 jit_solution(15772553551937544030)
XLA Ops:
  0.6 67.9 %schur_update.1 = (f32[2,4,16,256]{3,2,1,0:T(8,128)S(1)}, f32[4,4,16,256]{3,2,1,0:T(8,128)S(1)}) custom-call(s32[8]{0:T(128)} %bitcast.12, s32[8]{0:T(128)} %bitcast.13, s32[128]{0:T(128)} %reads_at.1, bf16[8,2,256,256]{3,2,1,0:T(8,128)(2,1)} %bitcast.9, bf16[8,1,256,256]{3,2,1,0:T(8,128)(2,1)} %bitcast.10, f32[2,4,16,256]{3,2,1,0:T(8,128)} %bitcast.11, ...), custom_call_target="tpu_custom_call" | custom-call | flops 536870912 | bytes 4194304 | tf_op jit(solution)/shard_map/schur_update/pallas_call | solution.py:378
  68.5 0.7 copy.11
  69.2 0.7 %copy.12 = f32[4,2,32,256]{3,2,1,0:T(8,128)} copy(f32[4,2,32,256]{3,2,1,0:T(8,128)S(1)} %bitcast.7) | data formatting | bytes 524288

commit v6 on v5

--- a/solution.py
+++ b/solution.py
@@ -85,16 +85,11 @@
 
     loads[2].wait()
     loads[3].wait()
-    lane = lax.broadcasted_iota(jnp.int32, (8, 128), 1)
-    sub = lax.broadcasted_iota(jnp.int32, (8, 128), 0)
-    down = jnp.zeros((8, 128), jnp.int32)
-    along = jnp.zeros((8, 128), jnp.int32)
+    lane = lax.broadcasted_iota(jnp.int32, (1, 128), 1)
+    along = jnp.zeros((1, 128), jnp.int32)
     for k in range(pairs):
-        group = owner[k] * per_dev + slot[k]
-        down = jnp.where(sub == k, group, down)
-        along = jnp.where(lane == f * pairs + k, group, along)
-    ids[y * F + f, 0:8, :] = down
-    ids[y * F + f, 8:16, :] = along
+        along = jnp.where(lane == f * pairs + k, owner[k] * per_dev + slot[k], along)
+    ids[y * F + f] = along
 
     def block_of(ff, yy):
         return yy // 2 * (2 * F) + ff * 2 + yy % 2
@@ -163,9 +158,10 @@
         return jnp.broadcast_to(jnp.where(at < 0, count, at), (8, 128))
 
     for yy in range(Y):
-        cols = ids[yy * F:(yy + 1) * F, 0:8, :].reshape(count, 128)
-        line = jnp.sum(ids[yy * F:(yy + 1) * F, 8:16, :], axis=0)
-        line = jnp.broadcast_to(line[None], (F, 8, 128)).reshape(count, 128)
+        line = sum(ids[yy * F + ff] for ff in range(F))
+        line = jnp.broadcast_to(line, (count, 128))
+        cols = jnp.sum(jnp.where(number == place, line, 0), axis=1, keepdims=True)
+        cols = jnp.broadcast_to(cols, (count, 128))
         meta_v[yy * 16:yy * 16 + 8, :] = latest((cols == line) & (number < place))
         meta_v[yy * 16 + 8:yy * 16 + 16, :] = latest(cols == place)
         sums[yy][count] = jnp.zeros((rows, HALF), jnp.float32)
@@ -339,7 +335,7 @@
         f32(*frontal.shape),
         f32(*diag_inverse.shape),
         f32(2, pairs, depth * width, HALF),
-        pltpu.VMEM((Y * F, 16, 128), jnp.int32),
+        pltpu.VMEM((Y * F, 1, 128), jnp.int32),
         pltpu.VMEM((Y * 16, 128), jnp.int32),
         pltpu.SMEM((Y * 16, 128), jnp.int32),
         f32(Y, per_dev, part, width),

time: 69.9 us -> 67.2 us (0.961)
  the two profiles are of different devices: /device:TPU:1 before, /device:TPU:22 now
where the time goes in v6:
time: 67.2 us; the launch traced here: 67.1 us
  Pallas kernels  65.1 us (97%)
  local copies, waits for them, and re-layouts  1.36 us (2%)
    pallas_call x1, Pallas kernels, per_device(): pl.pallas_call(kernel, out_shape=(pltpu.VMEM(frontal.shape, jnp.float32),...  65.1 us
    unnamed x2, local copies, waits for them, and re-layouts  1.36 us

profile of v6, /device:TPU:22, one launch (start us, length us, event | category | flops | bytes accessed | tf_op | source)
XLA Modules:
  0.0 67.1 jit_solution(10103160638209923074)
XLA Ops:
  0.6 65.1 %schur_update.1 = (f32[2,4,16,256]{3,2,1,0:T(8,128)S(1)}, f32[4,4,16,256]{3,2,1,0:T(8,128)S(1)}) custom-call(s32[8]{0:T(128)} %bitcast.12, s32[8]{0:T(128)} %bitcast.13, s32[128]{0:T(128)} %reads_at.1, bf16[8,2,256,256]{3,2,1,0:T(8,128)(2,1)} %bitcast.9, bf16[8,1,256,256]{3,2,1,0:T(8,128)(2,1)} %bitcast.10, f32[2,4,16,256]{3,2,1,0:T(8,128)} %bitcast.11, ...), custom_call_target="tpu_custom_call" | custom-call | flops 536870912 | bytes 4194304 | tf_op jit(solution)/shard_map/schur_update/pallas_call | solution.py:374
  65.7 0.7 copy.11
  66.4 0.7 %copy.12 = f32[4,2,32,256]{3,2,1,0:T(8,128)} copy(f32[4,2,32,256]{3,2,1,0:T(8,128)S(1)} %bitcast.7) | data formatting | bytes 524288
